TPU v7x, 32 devices: a whole 2x2x4 slice. The times are simulated.
32 devices in a mesh: rep: 4 (over y, core), shard: 8 (over z, x).
Axes of the slice: x: 2, y: 2, z: 4, core: 2. Of those that a mesh axis runs over, the one named last changes fastest.
Arguments:
- tokens: bfloat16 [8192, 768], P(('rep', 'shard')), may hold values from -6 to 6
- cotangent: bfloat16 [8192, 768], P(('rep', 'shard')), may hold values from -6 to 6
- segments: int32 [8192], P(('rep', 'shard')), may hold values from 1 to 24, as said below
- qkv_weight: float32 [768, 2304], P('shard'), may hold values from -0.21875 to 0.21875
- out_weight: float32 [768, 768], P('shard'), may hold values from -0.875 to 0.875
- up_weight: float32 [768, 3072], P('shard'), may hold values from -0.21875 to 0.21875
- down_weight: float32 [3072, 768], P('shard'), may hold values from -0.109375 to 0.109375
- small_weights: float32 [12, 768], P(None, 'shard'), may hold values from -1.2 to 1.6
- qkv_first: float32 [768, 2304], P('shard'), may hold values from -64 to 64
- out_first: float32 [768, 768], P('shard'), may hold values from -16 to 16
- up_first: float32 [768, 3072], P('shard'), may hold values from -16 to 16
- down_first: float32 [3072, 768], P('shard'), may hold values from -40 to 40
- small_first: float32 [12, 768], P(None, 'shard'), may hold values from -40 to 40
- qkv_second: float32 [768, 2304], P('shard'), may hold values from 245.76 to 3276.8
- out_second: float32 [768, 768], P('shard'), may hold values from 16.384 to 204.8
- up_second: float32 [768, 3072], P('shard'), may hold values from 24.576 to 294.912
- down_second: float32 [3072, 768], P('shard'), may hold values from 106.496 to 1392.64
- small_second: float32 [12, 768], P(None, 'shard'), may hold values from 122.88 to 1638.4
Outputs:
- mixed: bfloat16 [8192, 768], P(('rep', 'shard'))
- input_grad: float32 [8192, 768], P(('rep', 'shard'))
- qkv_next: float32 [768, 2304], P('shard')
- out_next: float32 [768, 768], P('shard')
- up_next: float32 [768, 3072], P('shard')
- down_next: float32 [3072, 768], P('shard')
- small_next: float32 [12, 768], P(None, 'shard')
- qkv_first_next: float32 [768, 2304], P('shard')
- out_first_next: float32 [768, 768], P('shard')
- up_first_next: float32 [768, 3072], P('shard')
- down_first_next: float32 [3072, 768], P('shard')
- small_first_next: float32 [12, 768], P(None, 'shard')
- qkv_second_next: float32 [768, 2304], P('shard')
- out_second_next: float32 [768, 768], P('shard')
- up_second_next: float32 [768, 3072], P('shard')
- down_second_next: float32 [3072, 768], P('shard')
- small_second_next: float32 [12, 768], P(None, 'shard')
Inputs may be any that keep to these rules, and one draw needn't show every extreme that they name: `segments`: rows are laid out as in the attention step: piece r of sequence s starts at row r * 2048 + s * 256. Along each sequence's positions the numbers never fall, and no two sequences share one; a document is a run of one number and holds at least 128 tokens; in every draw some sequence is a single document.
All inputs are finite; a program needn't handle non-finite values.
Results may differ from a plain program's by a relative error of at most 0.022.
Values may be sent and summed in bfloat16 or wider, within the bound.
No kernel may reach another device: no remote copies, remote signals or barrier semaphores. Data moves between devices by JAX's collectives and lax.ppermute only.
A program may use at most 192 MiB of HBM per device.

v0:
```python
import jax
import jax.numpy as jnp
from jax import lax
from jax.sharding import PartitionSpec as P

HEAD_DIM = 64
SPAN = 4
STEP_NUM = 10


NORM_EPS = 1e-05
BETA_ONE = 0.9
BETA_TWO = 0.95
ADAM_EPS = 1e-08
DECAY = 0.1
RATE_MATRIX = 0.05
RATE_SMALL = 0.3
MASKED = -1e30


def passed_along(block, axis, distance):
    devices = range(lax.axis_size(axis))
    route = [(i - distance, i) for i in devices if i - distance in devices]
    return lax.ppermute(block, axis, route)


def layer_norm(values, gain_row, bias_row):
    center = jnp.mean(values, axis=-1, keepdims=True)
    centered = values - center
    variance = jnp.mean(centered * centered, axis=-1, keepdims=True)
    return centered * lax.rsqrt(variance + NORM_EPS) * gain_row + bias_row


def smooth_unit(values):
    return jax.nn.gelu(values, approximate=False)


def unpack(packed):
    return (
        packed[0],
        packed[1],
        packed[2],
        packed[3],
        packed[4],
        packed[5],
        packed[6],
        packed[7],
        packed[8:].reshape(-1),
    )


def contract_rows(left_side, right_side):
    return lax.dot_general(
        left_side, right_side, (((0,), (0,)), ((), ())), preferred_element_type=jnp.float32
    )


def contract_cols(left_side, right_side):
    return lax.dot_general(
        left_side, right_side, (((1,), (1,)), ((), ())), preferred_element_type=jnp.float32
    )


def adam_update(master, gradient, moment_one, moment_two, step_rate):
    first_new = BETA_ONE * moment_one + (1.0 - BETA_ONE) * gradient
    second_new = BETA_TWO * moment_two + (1.0 - BETA_TWO) * gradient * gradient
    fix_one = 1.0 - BETA_ONE**STEP_NUM
    fix_two = 1.0 - BETA_TWO**STEP_NUM
    step_dir = first_new / fix_one / (jnp.sqrt(second_new / fix_two) + ADAM_EPS)
    return (master - step_rate * (step_dir + DECAY * master), first_new, second_new)


def local(
    tokens,
    cotangent,
    segments,
    qkv_weight,
    out_weight,
    up_weight,
    down_weight,
    small_weights,
    qkv_first,
    out_first,
    up_first,
    down_first,
    small_first,
    qkv_second,
    out_second,
    up_second,
    down_second,
    small_second,
):
    tok_rows = tokens.shape[0]
    model_width = tokens.shape[1]
    head_count = model_width // HEAD_DIM
    score_scale = HEAD_DIM ** (-0.5)
    low_qkv = qkv_weight.astype(jnp.bfloat16)
    low_out = out_weight.astype(jnp.bfloat16)
    low_up = up_weight.astype(jnp.bfloat16)
    low_down = down_weight.astype(jnp.bfloat16)
    low_small = small_weights.astype(jnp.bfloat16)
    gathered = (
        lax.all_gather(low_qkv, "shard", axis=0, tiled=True),
        lax.all_gather(low_out, "shard", axis=0, tiled=True),
        lax.all_gather(low_up, "shard", axis=0, tiled=True),
        lax.all_gather(low_down, "shard", axis=0, tiled=True),
        lax.all_gather(low_small, "shard", axis=1, tiled=True),
    )
    qkv_full, out_full, up_full, down_full, small_full = gathered
    gain_one, bias_one, query_bias, value_bias, out_bias, gain_two, bias_two, down_bias, up_bias = (
        unpack(small_full.astype(jnp.float32))
    )
    inputs = tokens.astype(jnp.float32)
    normed_one, norm_back_one = jax.vjp(layer_norm, inputs, gain_one, bias_one)
    hidden_one = normed_one.astype(jnp.bfloat16)
    joined_bias = jnp.concatenate([query_bias, jnp.zeros_like(query_bias), value_bias])
    projected = jnp.dot(hidden_one, qkv_full, preferred_element_type=jnp.float32) + joined_bias
    queries = (projected[:, :model_width] * score_scale).astype(jnp.bfloat16)
    key_values = projected[:, model_width:].astype(jnp.bfloat16)
    kv_blocks = [key_values]
    id_blocks = [segments]
    for offset in range(1, SPAN):
        kv_blocks.append(passed_along(key_values, "rep", offset))
        id_blocks.append(passed_along(segments, "rep", offset))
    all_kv = jnp.concatenate(kv_blocks, axis=0)
    key_ids = jnp.concatenate(id_blocks, axis=0)
    positions = jnp.arange(tok_rows)
    key_pos = jnp.concatenate([positions - offset * tok_rows for offset in range(SPAN)])
    allowed = (segments[:, None] == key_ids[None, :]) & (key_pos[None, :] <= positions[:, None])
    key_ones = jnp.ones((SPAN * tok_rows,), jnp.float32)

    def split_heads(block):
        keys_part = block[:, :model_width].reshape(-1, head_count, HEAD_DIM)
        values_part = block[:, model_width:].reshape(-1, head_count, HEAD_DIM)
        return (keys_part, values_part)

    query_heads = queries.reshape(tok_rows, head_count, HEAD_DIM)
    key_heads, value_heads = split_heads(all_kv)
    own_keys = key_values[:, :model_width].reshape(tok_rows, head_count, HEAD_DIM)
    self_score = jnp.einsum(
        "qhd,qhd->hq", query_heads, own_keys, preferred_element_type=jnp.float32
    )[:, :, None]
    scores = jnp.einsum("qhd,khd->hqk", query_heads, key_heads, preferred_element_type=jnp.float32)
    scores = jnp.where(allowed[None], scores, MASKED)
    exponent = jnp.exp(scores - self_score)
    row_total = jnp.einsum("hqk,k->hq", exponent, key_ones)[:, :, None]
    attn_probs = exponent / row_total
    log_total = self_score + jnp.log(row_total)
    mixed_heads = jnp.einsum(
        "hqk,khd->qhd",
        attn_probs.astype(jnp.bfloat16),
        value_heads,
        preferred_element_type=jnp.float32,
    )
    attended = mixed_heads.reshape(tok_rows, model_width).astype(jnp.bfloat16)
    residual = inputs + (jnp.dot(attended, out_full, preferred_element_type=jnp.float32) + out_bias)
    normed_two, norm_back_two = jax.vjp(layer_norm, residual, gain_two, bias_two)
    hidden_two = normed_two.astype(jnp.bfloat16)
    pre_act = jnp.dot(hidden_two, up_full, preferred_element_type=jnp.float32) + up_bias
    activated, act_back = jax.vjp(smooth_unit, pre_act)
    act_low = activated.astype(jnp.bfloat16)
    output = residual + (
        jnp.dot(act_low, down_full, preferred_element_type=jnp.float32) + down_bias
    )
    block_out = output.astype(jnp.bfloat16)
    qkv_back, out_back, up_back, down_back = (qkv_full, out_full, up_full, down_full)
    grad_out = cotangent.astype(jnp.float32)
    down_bias_grad = jnp.sum(grad_out, axis=0)
    down_grad = contract_rows(act_low, cotangent)
    act_grad = contract_cols(cotangent, down_back)
    pre_grad = act_back(act_grad)[0]
    pre_low = pre_grad.astype(jnp.bfloat16)
    up_bias_grad = jnp.sum(pre_low.astype(jnp.float32), axis=0)
    up_grad = contract_rows(hidden_two, pre_low)
    hidden_two_grad = contract_cols(pre_low, up_back)
    resid_back, gain_two_grad, bias_two_grad = norm_back_two(hidden_two_grad)
    resid_grad = grad_out + resid_back
    branch_low = resid_grad.astype(jnp.bfloat16)
    out_bias_grad = jnp.sum(branch_low.astype(jnp.float32), axis=0)
    out_grad = contract_rows(attended, branch_low)
    attended_grad = (
        contract_cols(branch_low, out_back)
        .astype(jnp.bfloat16)
        .reshape(tok_rows, head_count, HEAD_DIM)
    )
    key_heads_back, value_heads_back = split_heads(all_kv)
    scores_again = jnp.einsum(
        "qhd,khd->hqk", query_heads, key_heads_back, preferred_element_type=jnp.float32
    )
    scores_again = jnp.where(allowed[None], scores_again, MASKED)
    probs_again = jnp.exp(scores_again - log_total)
    prob_grad = jnp.einsum(
        "qhd,khd->hqk", attended_grad, value_heads_back, preferred_element_type=jnp.float32
    )
    value_grad = jnp.einsum(
        "hqk,qhd->khd",
        probs_again.astype(jnp.bfloat16),
        attended_grad,
        preferred_element_type=jnp.float32,
    )
    inner_sum = jnp.einsum("hqk,hqk->hq", prob_grad, probs_again)[:, :, None]
    score_grad = (probs_again * (prob_grad - inner_sum)).astype(jnp.bfloat16)
    query_grad = (
        jnp.einsum(
            "hqk,khd->qhd", score_grad, key_heads_back, preferred_element_type=jnp.float32
        ).reshape(tok_rows, model_width)
        * score_scale
    )
    key_grad = jnp.einsum(
        "hqk,qhd->khd", score_grad, query_heads, preferred_element_type=jnp.float32
    )
    kv_grad = jnp.concatenate(
        [key_grad.reshape(-1, model_width), value_grad.reshape(-1, model_width)], axis=1
    )
    own_grad = kv_grad[:tok_rows]
    for offset in range(1, SPAN):
        own_grad = own_grad + passed_along(
            kv_grad[offset * tok_rows : (offset + 1) * tok_rows].astype(jnp.bfloat16),
            "rep",
            -offset,
        ).astype(jnp.float32)
    proj_low = jnp.concatenate([query_grad, own_grad], axis=1).astype(jnp.bfloat16)
    proj_wide = proj_low.astype(jnp.float32)
    query_bias_grad = jnp.sum(proj_wide[:, :model_width], axis=0)
    value_bias_grad = jnp.sum(proj_wide[:, 2 * model_width :], axis=0)
    qkv_grad = contract_rows(hidden_one, proj_low)
    hidden_one_grad = contract_cols(proj_low, qkv_back)
    input_back, gain_one_grad, bias_one_grad = norm_back_one(hidden_one_grad)
    input_grad = resid_grad + input_back
    vector_grads = jnp.stack(
        [
            gain_one_grad,
            bias_one_grad,
            query_bias_grad,
            value_bias_grad,
            out_bias_grad,
            gain_two_grad,
            bias_two_grad,
            down_bias_grad,
        ]
    )
    small_grad = jnp.concatenate([vector_grads, up_bias_grad.reshape(-1, model_width)], axis=0)
    owned = (
        lax.psum_scatter(qkv_grad, "shard", scatter_dimension=0, tiled=True),
        lax.psum_scatter(out_grad, "shard", scatter_dimension=0, tiled=True),
        lax.psum_scatter(up_grad, "shard", scatter_dimension=0, tiled=True),
        lax.psum_scatter(down_grad, "shard", scatter_dimension=0, tiled=True),
        lax.psum_scatter(small_grad, "shard", scatter_dimension=1, tiled=True),
    )
    summed = (
        lax.psum(owned[0].astype(jnp.bfloat16), "rep").astype(jnp.float32),
        lax.psum(owned[1].astype(jnp.bfloat16), "rep").astype(jnp.float32),
        lax.psum(owned[2].astype(jnp.bfloat16), "rep").astype(jnp.float32),
        lax.psum(owned[3].astype(jnp.bfloat16), "rep").astype(jnp.float32),
        lax.psum(owned[4].astype(jnp.bfloat16), "rep").astype(jnp.float32),
    )
    qkv_res = adam_update(qkv_weight, summed[0], qkv_first, qkv_second, RATE_MATRIX)
    out_res = adam_update(out_weight, summed[1], out_first, out_second, RATE_MATRIX)
    up_res = adam_update(up_weight, summed[2], up_first, up_second, RATE_MATRIX)
    down_res = adam_update(down_weight, summed[3], down_first, down_second, RATE_MATRIX)
    small_res = adam_update(small_weights, summed[4], small_first, small_second, RATE_SMALL)
    return (
        block_out,
        input_grad,
        qkv_res[0],
        out_res[0],
        up_res[0],
        down_res[0],
        small_res[0],
        qkv_res[1],
        out_res[1],
        up_res[1],
        down_res[1],
        small_res[1],
        qkv_res[2],
        out_res[2],
        up_res[2],
        down_res[2],
        small_res[2],
    )


def solution(mesh):
    return jax.shard_map(
        local,
        mesh=mesh,
        in_specs=(
            P(("rep", "shard"), None),
            P(("rep", "shard"), None),
            P(("rep", "shard")),
            P("shard", None),
            P("shard", None),
            P("shard", None),
            P("shard", None),
            P(None, "shard"),
            P("shard", None),
            P("shard", None),
            P("shard", None),
            P("shard", None),
            P(None, "shard"),
            P("shard", None),
            P("shard", None),
            P("shard", None),
            P("shard", None),
            P(None, "shard"),
        ),
        out_specs=(
            P(("rep", "shard"), None),
            P(("rep", "shard"), None),
            P("shard", None),
            P("shard", None),
            P("shard", None),
            P("shard", None),
            P(None, "shard"),
            P("shard", None),
            P("shard", None),
            P("shard", None),
            P("shard", None),
            P(None, "shard"),
            P("shard", None),
            P("shard", None),
            P("shard", None),
            P("shard", None),
            P(None, "shard"),
        ),
        check_vma=False,
    )
```

profile of v0, /device:TPU:11, one launch (start us, length us, event | category | flops | bytes accessed | tf_op | source)
XLA Modules:
  0.0 965.1 jit_solution(1156299705373759662)
XLA Ops:
  7.3 2.1 convert_element_type.123
  12.2 3.1 collective-permute-start.4
  15.4 1.9 collective-permute-start.3
  18.9 22.0 %all-gather = bf16[8,96,12]{1,2,0:T(8,128)(2,1)S(1)} all-gather(bf16[1,96,12]{1,2,0:T(8,128)(2,1)S(1)} %convert_bitcast_fusion), channel_id=1, replica_groups=mesh['rep'=4,'shard'=8] {'shard'}, dimensions={0}, use_global_device_ids=true | all-gather | bytes 20736 | tf_op jit(solution)/shard_map/all_gather | solution.py:107
  42.1 32.8 %all-gather.6.cloned.1.call-done = bf16[768,2304]{1,0:T(8,128)(2,1)} async-done(((bf16[96,2304]{1,0:T(8,128)(2,1)}), bf16[768,2304]{1,0:T(8,128)(2,1)}) %all-gather.6.cloned.1.call-update) | async-done | bytes 3538960 | tf_op jit(solution)/shard_map/all_gather | solution.py:103
  75.0 4.6 fusion.85
  82.0 3.7 collective-permute-start.1
  85.8 2.5 collective-permute-start
  90.4 12.1 %collective-permute-done.1 = bf16[256,1536]{1,0:T(8,128)(2,1)} collective-permute-done((bf16[256,1536]{1,0:T(8,128)(2,1)}, bf16[256,1536]{1,0:T(8,128)(2,1)}, u32[]{:S(2)}, u32[]{:S(2)}) %collective-permute-start.1) | collective-permute-done | bytes 786464 | tf_op jit(solution)/shard_map/ppermute | solution.py:24
  102.5 16.2 %collective-permute-done = bf16[256,1536]{1,0:T(8,128)(2,1)} collective-permute-done((bf16[256,1536]{1,0:T(8,128)(2,1)}, bf16[256,1536]{1,0:T(8,128)(2,1)}, u32[]{:S(2)}, u32[]{:S(2)}) %collective-permute-start) | collective-permute-done | bytes 786464 | tf_op jit(solution)/shard_map/ppermute | solution.py:24
  118.7 2.1 pad_maximum_fusion.1
  124.3 3.2 copy.56
  127.5 1.8 fusion.87
  129.4 2.7 fusion
  132.0 2.1 copy-done
  134.1 3.7 fusion.27
  137.9 2.0 fusion.86
  140.1 58.1 %all-gather.10.cloned.1.call-done = bf16[768,3072]{1,0:T(8,128)(2,1)} async-done(((bf16[96,3072]{1,0:T(8,128)(2,1)}), bf16[768,3072]{1,0:T(8,128)(2,1)}) %all-gather.10.cloned.1.call-update) | async-done | bytes 4718608 | tf_op jit(solution)/shard_map/all_gather | solution.py:105
  198.3 5.5 convolution_add_fusion.1
  203.8 75.1 %all-gather.12.cloned.1.call-done = bf16[3072,768]{1,0:T(8,128)(2,1)} async-done(((bf16[384,768]{1,0:T(8,128)(2,1)}), bf16[3072,768]{1,0:T(8,128)(2,1)}) %all-gather.12.cloned.1.call-update) | async-done | bytes 4718608 | tf_op jit(solution)/shard_map/all_gather | solution.py:106
  278.9 11.8 %convert_reduce_fusion = (f32[3072]{0:T(1024)S(1)}, bf16[256,3072]{1,0:T(8,128)(2,1)S(1)}, f32[256,3072]{1,0:T(8,128)}) fusion(f32[256,3072]{1,0:T(8,128)} %convolution_add_fusion.1, bf16[256,768]{1,0:T(8,128)(2,1)S(1)} %copy-done.15, bf16[3072,768]{1,0:T(8,128)(2,1)} %all-gather.12.cloned.1.call-done), kind=kOutput, calls=%fused_computation.24 | convolution fusion | flops 1266152448 | bytes 12988416 | tf_op jit(solution)/shard_map/dot_general | solution.py:59
  293.4 1.9 fusion.89
  297.4 11.8 %multiply_reduce_fusion = (f32[12,256]{1,0:T(8,128)S(1)}, f32[12,256,1024]{2,1,0:T(8,128)}) fusion(f32[12,256,1024]{2,1,0:T(8,128)} %copy-done, f32[12,256]{1,0:T(8,128)S(1)} %log_add_fusion, pred[256,1024]{1,0:T(8,128)(4,1)S(1)} %fusion.36, bf16[256,12,64]{0,2,1:T(8,128)(2,1)S(1)} %bitcast.82, bf16[1024,12,64]{0,2,1:T(8,128)(2,1)} %bitcast.77), kind=kOutput, calls=%fused_computation | convolution fusion | flops 415233024 | bytes 27418624 | tf_op jit(solution)/shard_map/qhd,khd->hqk/dot_general | solution.py:192
  310.6 6.6 multiply_convert_fusion
  318.4 2.8 fusion.3
  321.9 3.7 collective-permute-start.6
  328.1 2.0 fusion.26
  330.1 13.7 %collective-permute-done.6 = bf16[256,1536]{0,1:T(8,128)(2,1)S(1)} collective-permute-done((bf16[256,1536]{0,1:T(8,128)(2,1)S(1)}, bf16[256,1536]{0,1:T(8,128)(2,1)S(1)}, u32[]{:S(2)}, u32[]{:S(2)}) %collective-permute-start.6) | collective-permute-done | bytes 786464 | tf_op jit(solution)/shard_map/ppermute | solution.py:24
  343.8 18.2 %collective-permute-done.7 = bf16[256,1536]{0,1:T(8,128)(2,1)S(1)} collective-permute-done((bf16[256,1536]{0,1:T(8,128)(2,1)S(1)}, bf16[256,1536]{0,1:T(8,128)(2,1)S(1)}, u32[]{:S(2)}, u32[]{:S(2)}) %collective-permute-start.7) | collective-permute-done | bytes 786464 | tf_op jit(solution)/shard_map/ppermute | solution.py:24
  363.4 5.4 fusion.50
  370.5 5.2 fusion.68
  375.7 4.0 multiply_convert_fusion.1
  379.8 5.1 fusion.90
  385.0 3.7 fusion.69
  394.9 103.1 %reduce-scatter.8.cloned.1.call-done = f32[96,2304]{1,0:T(8,128)} async-done(((f32[768,2304]{1,0:T(8,128)}), f32[96,2304]{1,0:T(8,128)}) %reduce-scatter.8.cloned.1.call-update) | async-done | bytes 884752 | tf_op jit(solution)/shard_map/reduce_scatter | solution.py:244
  498.0 2.0 convert_element_type.144
  500.0 164.2 %reduce-scatter.12.cloned.1.call-done = f32[96,3072]{1,0:T(8,128)} async-done(((f32[768,3072]{1,0:T(8,128)}), f32[96,3072]{1,0:T(8,128)}) %reduce-scatter.12.cloned.1.call-update) | async-done | bytes 1179664 | tf_op jit(solution)/shard_map/reduce_scatter | solution.py:246
  664.2 2.2 convert_element_type.148
  666.3 164.4 %reduce-scatter.14.cloned.1.call-done = f32[384,768]{1,0:T(8,128)} async-done(((f32[3072,768]{1,0:T(8,128)}), f32[384,768]{1,0:T(8,128)}) %reduce-scatter.14.cloned.1.call-update) | async-done | bytes 1179664 | tf_op jit(solution)/shard_map/reduce_scatter | solution.py:247
  830.8 2.1 convert_element_type.150
  833.0 4.6 fusion.25
  837.5 57.2 %reduce-scatter.16.cloned.1.call-done = f32[96,12]{1,0:T(8,128)} async-done(((f32[768,12]{1,0:T(8,128)}), f32[96,12]{1,0:T(8,128)}) %reduce-scatter.16.cloned.1.call-update) | async-done | bytes 4624
  895.6 8.1 psum.39
  905.0 41.4 %all-reduce.3.cloned.1.call-done = (bf16[96,2304]{1,0:T(8,128)(2,1)}, bf16[96,768]{1,0:T(8,128)(2,1)}, bf16[96,3072]{1,0:T(8,128)(2,1)}, bf16[384,768]{1,0:T(8,128)(2,1)}) async-done(((bf16[96,2304]{1,0:T(8,128)(2,1)}, bf16[96,768]{1,0:T(8,128)(2,1)}, bf16[96,3072]{1,0:T(8,128)(2,1)}, bf16[384,768]{1,0:T(8,128)(2,1)}), (bf16[96,2304]{1,0:T(8,128)(2,1)}, bf16[96,768]{1,0:T(8,128)(2,1)}, ...) | async-done | bytes 1769488 | tf_op jit(solution)/shard_map/psum | solution.py:251
  946.4 2.2 multiply_subtract_fusion.3
  948.6 3.6 multiply_subtract_fusion.2
  952.3 2.4 multiply_subtract_fusion.1
  955.6 2.4 multiply_subtract_fusion
  (176 shorter events, 36.5 us)
Async XLA Ops:
  7.2 4.1 copy-start.9
  7.2 5.0 copy-start.35
  7.2 10.8 %copy-start.11 = (f32[384,768]{1,0:T(8,128)S(1)}, f32[384,768]{1,0:T(8,128)}, u32[]{:S(2)}) copy-start(f32[384,768]{1,0:T(8,128)} %param.24) | copy-start | bytes 3538948
  7.2 67.7 %all-gather.6.cloned.1.call-start = ((), (), s32[]{:S(2)}) async-start(), calls=%async_computation.5 | async-start | bytes 3981312 | tf_op jit(solution)/shard_map/all_gather | solution.py:103
  9.4 9.5 copy-start.33
  9.4 32.3 %copy-start.1 = (bf16[256,768]{1,0:T(8,128)(2,1)S(1)}, bf16[256,768]{1,0:T(8,128)(2,1)}, u32[]{:S(2)}) copy-start(bf16[256,768]{1,0:T(8,128)(2,1)} %param.18) | copy-start | bytes 1179652
  9.4 128.4 %all-gather.8.cloned.1.call-start = ((), (), s32[]{:S(2)}) async-start(), calls=%async_computation.6 | async-start | bytes 1327104 | tf_op jit(solution)/shard_map/all_gather | solution.py:104
  11.2 187.1 %all-gather.10.cloned.1.call-start = ((), (), s32[]{:S(2)}) async-start(), calls=%async_computation.7 | async-start | bytes 5308416 | tf_op jit(solution)/shard_map/all_gather | solution.py:105
  12.2 266.8 %all-gather.12.cloned.1.call-start = ((), (), s32[]{:S(2)}) async-start(), calls=%async_computation.8 | async-start | bytes 5308416 | tf_op jit(solution)/shard_map/all_gather | solution.py:106
  12.2 73.6 %collective-permute-start.4 = (s32[256]{0:T(256)S(1)}, s32[256]{0:T(256)S(1)}, u32[]{:S(2)}, u32[]{:S(2)}) collective-permute-start(s32[256]{0:T(256)S(1)} %copy-done.35), channel_id=1, source_target_pairs={{0,16},{8,24},{1,17},{9,25},{2,18},{10,26},{3,19},{11,27},{4,20},{... | collective-permute-start | bytes 3080 | tf_op jit(solution)/shard_map/ppermute | solution.py:24
  15.4 73.0 %collective-permute-start.3 = (s32[256]{0:T(256)S(1)}, s32[256]{0:T(256)S(1)}, u32[]{:S(2)}, u32[]{:S(2)}) collective-permute-start(s32[256]{0:T(256)S(1)} %copy-done.35), channel_id=1, source_target_pairs={{0,8},{8,16},{16,24},{1,9},{9,17},{17,25},{2,10},{10,18},{18,26},{... | collective-permute-start | bytes 3080 | tf_op jit(solution)/shard_map/ppermute | solution.py:24
  17.3 71.0 %collective-permute-start.5 = (s32[256]{0:T(256)S(1)}, s32[256]{0:T(256)S(1)}, u32[]{:S(2)}, u32[]{:S(2)}) collective-permute-start(s32[256]{0:T(256)S(1)} %copy-done.35), channel_id=1, source_target_pairs={{0,24},{1,25},{2,26},{3,27},{4,28},{5,29},{6,30},{7,31}} | collective-permute-start | bytes 3080 | tf_op jit(solution)/shard_map/ppermute | solution.py:24
  18.9 374.4 %reduce-scatter.10.cloned.1.call-start = ((), (), s32[]{:S(2)}) async-start(), calls=%async_computation.10 | async-start | bytes 2654208 | tf_op jit(solution)/shard_map/reduce_scatter | solution.py:245
  80.5 9.9 %collective-permute-start.2 = (bf16[256,1536]{1,0:T(8,128)(2,1)}, bf16[256,1536]{1,0:T(8,128)(2,1)}, u32[]{:S(2)}, u32[]{:S(2)}) collective-permute-start(bf16[256,1536]{1,0:T(8,128)(2,1)} %slice.91), channel_id=1, source_target_pairs={{0,24},{1,25},{2,26},{3,27},{4,28},{5,29},{6,30},{7,31}} | collective-permute-start | bytes 2359304 | tf_op jit(solution)/shard_map/ppermute | solution.py:24
  82.0 20.5 %collective-permute-start.1 = (bf16[256,1536]{1,0:T(8,128)(2,1)}, bf16[256,1536]{1,0:T(8,128)(2,1)}, u32[]{:S(2)}, u32[]{:S(2)}) collective-permute-start(bf16[256,1536]{1,0:T(8,128)(2,1)} %slice.91), channel_id=1, source_target_pairs={{0,16},{8,24},{1,17},{9,25},{2,18},{10,26},{3,19},{11,27},{4,20},{... | collective-permute-start | bytes 2359304 | tf_op jit(solution)/shard_map/ppermute | solution.py:24
  85.8 32.9 %collective-permute-start = (bf16[256,1536]{1,0:T(8,128)(2,1)}, bf16[256,1536]{1,0:T(8,128)(2,1)}, u32[]{:S(2)}, u32[]{:S(2)}) collective-permute-start(bf16[256,1536]{1,0:T(8,128)(2,1)} %slice.91), channel_id=1, source_target_pairs={{0,8},{8,16},{16,24},{1,9},{9,17},{17,25},{2,10},{10,18},{18,26},{... | collective-permute-start | bytes 2359304 | tf_op jit(solution)/shard_map/ppermute | solution.py:24
  88.6 220.6 %copy-start.13 = (pred[256,1024]{1,0:T(8,128)(4,1)}, pred[256,1024]{1,0:T(8,128)(4,1)S(1)}, u32[]{:S(2)}) copy-start(pred[256,1024]{1,0:T(8,128)(4,1)S(1)} %fusion.36) | copy-start | bytes 786436
  124.3 5.0 copy-start.2
  129.3 4.8 copy-start
  129.3 4.8 copy-start.8
  137.8 60.4 %copy-start.22 = (bf16[12,64,256]{2,1,0:T(8,128)(2,1)}, bf16[12,64,256]{2,1,0:T(8,128)(2,1)S(1)}, u32[]{:S(2)}) copy-start(bf16[12,64,256]{2,1,0:T(8,128)(2,1)S(1)} %fusion.27) | copy-start | bytes 1179652
  139.9 152.6 %copy-start.4 = (f32[256,768]{1,0:T(8,128)}, f32[256,768]{1,0:T(8,128)S(1)}, u32[]{:S(2)}) copy-start(f32[256,768]{1,0:T(8,128)S(1)} %get-tuple-element.70) | copy-start | bytes 2359300
  198.3 80.7 %copy-start.15 = (bf16[256,768]{1,0:T(8,128)(2,1)S(1)}, bf16[256,768]{1,0:T(8,128)(2,1)}, u32[]{:S(2)}) copy-start(bf16[256,768]{1,0:T(8,128)(2,1)} %param.19) | copy-start | bytes 1179652
  278.9 11.8 %copy-start.36 = (bf16[768,3072]{1,0:T(8,128)(2,1)S(1)}, bf16[768,3072]{1,0:T(8,128)(2,1)}, u32[]{:S(2)}) copy-start(bf16[768,3072]{1,0:T(8,128)(2,1)} %all-gather.10.cloned.1.call-done) | copy-start | bytes 14155780
  292.8 4.3 copy-start.6
  297.3 11.9 %copy-start.20 = (bf16[256,768]{0,1:T(8,128)(2,1)}, bf16[256,768]{0,1:T(8,128)(2,1)S(1)}, u32[]{:S(2)}) copy-start(bf16[256,768]{0,1:T(8,128)(2,1)S(1)} %copy.60) | copy-start | bytes 1179652
  297.3 200.6 %reduce-scatter.8.cloned.1.call-start = ((), (), s32[]{:S(2)}) async-start(), calls=%async_computation.9 | async-start | bytes 7962624 | tf_op jit(solution)/shard_map/reduce_scatter | solution.py:244
  297.4 11.9 %slice-start = ((s8[12582912]{0:T(1024)(128)(4,1)}), s8[4194304]{0:T(1024)(128)(4,1)S(1)}, s32[]{:S(2)}) async-start(s8[12582912]{0:T(1024)(128)(4,1)} %bitcast.66), calls=%async_computation.15 | async-start | bytes 8388608
  297.4 11.8 %slice-start.1 = ((s8[12582912]{0:T(1024)(128)(4,1)}), s8[4194304]{0:T(1024)(128)(4,1)S(1)}, s32[]{:S(2)}) async-start(s8[12582912]{0:T(1024)(128)(4,1)} %bitcast.66), calls=%async_computation.16 | async-start | bytes 8388608
  297.4 13.1 %slice-start.2 = ((s8[12582912]{0:T(1024)(128)(4,1)}), s8[4194304]{0:T(1024)(128)(4,1)S(1)}, s32[]{:S(2)}) async-start(s8[12582912]{0:T(1024)(128)(4,1)} %bitcast.66), calls=%async_computation.17 | async-start | bytes 8388608
  321.8 6.3 copy-start.3
  321.9 21.9 %collective-permute-start.6 = (bf16[256,1536]{0,1:T(8,128)(2,1)S(1)}, bf16[256,1536]{0,1:T(8,128)(2,1)S(1)}, u32[]{:S(2)}, u32[]{:S(2)}) collective-permute-start(bf16[256,1536]{0,1:T(8,128)(2,1)S(1)} %get-tuple-element.60), channel_id=1, source_target_pairs={{8,0},{16,8},{24,16},{9,1},{17,9},{25,17},{10,2},{18,10},{26,18},{... | collective-permute-start | bytes 2359304 | tf_op jit(solution)/shard_map/ppermute | solution.py:24
  325.7 18.2 %collective-permute-start.8 = (bf16[256,1536]{0,1:T(8,128)(2,1)S(1)}, bf16[256,1536]{0,1:T(8,128)(2,1)S(1)}, u32[]{:S(2)}, u32[]{:S(2)}) collective-permute-start(bf16[256,1536]{0,1:T(8,128)(2,1)S(1)} %get-tuple-element.61), channel_id=1, source_target_pairs={{24,0},{25,1},{26,2},{27,3},{28,4},{29,5},{30,6},{31,7}} | collective-permute-start | bytes 2359304 | tf_op jit(solution)/shard_map/ppermute | solution.py:24
  326.4 35.7 %collective-permute-start.7 = (bf16[256,1536]{0,1:T(8,128)(2,1)S(1)}, bf16[256,1536]{0,1:T(8,128)(2,1)S(1)}, u32[]{:S(2)}, u32[]{:S(2)}) collective-permute-start(bf16[256,1536]{0,1:T(8,128)(2,1)S(1)} %get-tuple-element.62), channel_id=1, source_target_pairs={{16,0},{24,8},{17,1},{25,9},{18,2},{26,10},{19,3},{27,11},{20,4},{... | collective-permute-start | bytes 2359304 | tf_op jit(solution)/shard_map/ppermute | solution.py:24
  330.1 33.3 %copy-start.17 = (bf16[12,64,256]{2,1,0:T(8,128)(2,1)}, bf16[12,64,256]{2,1,0:T(8,128)(2,1)S(1)}, u32[]{:S(2)}) copy-start(bf16[12,64,256]{2,1,0:T(8,128)(2,1)S(1)} %fusion.26) | copy-start | bytes 1179652
  368.8 295.3 %reduce-scatter.12.cloned.1.call-start = ((), (), s32[]{:S(2)}) async-start(), calls=%async_computation.11 | async-start | bytes 10616832 | tf_op jit(solution)/shard_map/reduce_scatter | solution.py:246
  375.7 455.1 %reduce-scatter.14.cloned.1.call-start = ((), (), s32[]{:S(2)}) async-start(), calls=%async_computation.12 | async-start | bytes 10616832 | tf_op jit(solution)/shard_map/reduce_scatter | solution.py:247
  375.7 4.0 copy-start.16
  384.9 509.8 %reduce-scatter.16.cloned.1.call-start = ((), (), s32[]{:S(2)}) async-start(), calls=%async_computation.13 | async-start | bytes 442368
  385.0 4.2 copy-start.7
  393.2 553.2 %all-reduce.3.cloned.1.call-start = ((), (), s32[]{:S(2)}) async-start(), calls=%async_computation.14 | async-start | bytes 3538944 | tf_op jit(solution)/shard_map/psum | solution.py:251
  832.9 70.7 %copy-start.34 = (f32[12,96]{1,0:T(8,128)S(1)}, f32[12,96]{1,0:T(8,128)}, u32[]{:S(2)}) copy-start(f32[12,96]{1,0:T(8,128)} %param.30) | copy-start | bytes 13828
  833.0 113.4 %copy-start.26 = (f32[96,768]{1,0:T(8,128)S(1)}, f32[96,768]{1,0:T(8,128)}, u32[]{:S(2)}) copy-start(f32[96,768]{1,0:T(8,128)} %param.22) | copy-start | bytes 884740
  833.0 115.6 %copy-start.19 = (f32[96,2304]{1,0:T(8,128)S(1)}, f32[96,2304]{1,0:T(8,128)}, u32[]{:S(2)}) copy-start(f32[96,2304]{1,0:T(8,128)} %param.21) | copy-start | bytes 2654212
  948.5 3.7 copy-start.10
  948.5 3.7 copy-start.27
  948.5 3.7 copy-start.28
  948.6 3.7 copy-start.32
  (11 other events, 21.3 us)
Sparse Core Ops, SparseCore 0:
  10.8 64.0 all-gather.5
  77.7 39.6 all-gather.7
  120.1 78.0 all-gather.9
  200.9 78.0 all-gather.11
  297.5 67.3 reduce-scatter.9
  369.0 128.9 reduce-scatter.7
  502.0 162.1 reduce-scatter.11
  668.2 162.5 reduce-scatter.13
  835.0 59.6 reduce-scatter.15
  898.5 47.8 all-reduce.2
where the time goes:
time: 971 us; the launch traced here: 965 us
  waiting for transfers between devices  757 us (78%)
  matrix products  79.2 us (8%)
  other arithmetic  46.2 us (5%)
  blocking collectives  30.1 us (3%)
  starting transfers between devices  20.1 us (2%)
  local copies, waits for them, and re-layouts  17.5 us (2%)
  between operations  15.2 us (2%)
    reduce_scatter x1, waiting for transfers between devices, local(): lax.psum_scatter(down_grad, 'shard', scatter_dimension=0, tiled=True)  164 us
    reduce_scatter x1, waiting for transfers between devices, local(): lax.psum_scatter(up_grad, 'shard', scatter_dimension=0, tiled=True)  164 us
    reduce_scatter x1, waiting for transfers between devices, local(): lax.psum_scatter(qkv_grad, 'shard', scatter_dimension=0, tiled=True)  103 us
    all_gather x1, waiting for transfers between devices, local(): lax.all_gather(low_down, 'shard', axis=0, tiled=True)  75.1 us
    ppermute x9, waiting for transfers between devices, passed_along(): return lax.ppermute(block, axis, route)  60.2 us
    all_gather x1, waiting for transfers between devices, local(): lax.all_gather(low_up, 'shard', axis=0, tiled=True)  58.1 us
    unnamed x11, waiting for transfers between devices  57.3 us
    psum x1, waiting for transfers between devices, local(): lax.psum(owned[0].astype(jnp.bfloat16), 'rep').astype(jnp.float32)  41.4 us
  transfers between devices with their start and end apart: 19, of which 12 were waited for; matrix products, arithmetic and copies ran while one was open for 11% of the time, Pallas kernels for 0%

commit v1 on v0

v1 whole, which is shorter than its diff:
```python
import jax
import jax.numpy as jnp
from jax import lax
from jax.experimental import pallas as pl
from jax.experimental.pallas import tpu as pltpu
from jax.sharding import PartitionSpec as P

HEAD_DIM = 64
SPAN = 4
STEP_NUM = 10


NORM_EPS = 1e-05
BETA_ONE = 0.9
BETA_TWO = 0.95
ADAM_EPS = 1e-08
DECAY = 0.1
RATE_MATRIX = 0.05
RATE_SMALL = 0.3
MASKED = -1e30
BLOCK = 256
F32 = jnp.float32
BF16 = jnp.bfloat16


def swapped(block, bit):
    return lax.ppermute(block, "rep", [(i, i ^ bit) for i in range(SPAN)])


def rep_gather(block):
    rep = lax.axis_index("rep")
    far = swapped(block, 2)
    near = swapped(block, 1)
    cross = swapped(far, 1)
    odd = (rep & 1) == 1
    high = (rep & 2) == 2
    low_pair = (jnp.where(odd, near, block), jnp.where(odd, block, near))
    high_pair = (jnp.where(odd, cross, far), jnp.where(odd, far, cross))
    return (
        jnp.where(high, high_pair[0], low_pair[0]),
        jnp.where(high, high_pair[1], low_pair[1]),
        jnp.where(high, low_pair[0], high_pair[0]),
        jnp.where(high, low_pair[1], high_pair[1]),
    )


def rep_scatter(partial):
    rep = lax.axis_index("rep")
    rows = partial.shape[0] // SPAN

    def piece(index):
        return lax.dynamic_slice_in_dim(partial, index * rows, rows, 0)

    near_send = jnp.concatenate([piece(rep ^ 3), piece(rep ^ 1)], axis=0).astype(BF16)
    near = swapped(near_send, 1).astype(F32)
    far_send = (piece(rep ^ 2) + near[:rows]).astype(BF16)
    return piece(rep) + near[rows:] + swapped(far_send, 2).astype(F32)


def norm_parts(values):
    center = jnp.mean(values, axis=-1, keepdims=True)
    centered = values - center
    variance = jnp.mean(centered * centered, axis=-1, keepdims=True)
    inverse = lax.rsqrt(variance + NORM_EPS)
    return centered * inverse, inverse


def norm_back(normalized, inverse, gain, grad):
    scaled = grad * gain
    mean_one = jnp.mean(scaled, axis=-1, keepdims=True)
    mean_two = jnp.mean(scaled * normalized, axis=-1, keepdims=True)
    return inverse * (scaled - mean_one - normalized * mean_two)


def contract_rows(left_side, right_side):
    return lax.dot_general(
        left_side, right_side, (((0,), (0,)), ((), ())), preferred_element_type=F32
    )


def contract_cols(left_side, right_side):
    return lax.dot_general(
        left_side, right_side, (((1,), (1,)), ((), ())), preferred_element_type=F32
    )


def adam_update(master, gradient, moment_one, moment_two, step_rate):
    first_new = BETA_ONE * moment_one + (1.0 - BETA_ONE) * gradient
    second_new = BETA_TWO * moment_two + (1.0 - BETA_TWO) * gradient * gradient
    fix_one = 1.0 - BETA_ONE**STEP_NUM
    fix_two = 1.0 - BETA_TWO**STEP_NUM
    step_dir = first_new / fix_one / (jnp.sqrt(second_new / fix_two) + ADAM_EPS)
    return (master - step_rate * (step_dir + DECAY * master), first_new, second_new)


def mask_bias(seg_col_ref, seg_row_ref, start, keys):
    same = seg_col_ref[:keys, :] == seg_row_ref[:, start : start + BLOCK]
    key_at = lax.broadcasted_iota(jnp.int32, (keys, BLOCK), 0)
    query_at = lax.broadcasted_iota(jnp.int32, (keys, BLOCK), 1) + start
    return jnp.where(same & (key_at <= query_at), 0.0, MASKED)


def head_lanes(shape, head):
    lane = lax.broadcasted_iota(jnp.int32, shape, 1)
    return (lane >= head * HEAD_DIM) & (lane < (head + 1) * HEAD_DIM)


def attend_kernel(q_ref, k_ref, v_ref, seg_col_ref, seg_row_ref, out_ref, lse_ref):
    total, width = q_ref.shape
    heads = width // HEAD_DIM
    value_t = v_ref[...].T
    lse_ref[...] = jnp.zeros_like(lse_ref)
    for start in range(0, total, BLOCK):
        keys = start + BLOCK
        bias = mask_bias(seg_col_ref, seg_row_ref, start, keys)
        query = q_ref[start : start + BLOCK, :]
        pieces = []
        for head in range(heads):
            masked = jnp.where(head_lanes(query.shape, head), query, 0)
            scores = contract_cols(k_ref[:keys, :], masked) + bias
            peak = jnp.max(scores, axis=0, keepdims=True)
            exponent = jnp.exp(scores - peak)
            row_total = jnp.sum(exponent, axis=0, keepdims=True)
            mixed = jnp.dot(
                value_t[head * HEAD_DIM : (head + 1) * HEAD_DIM, :keys],
                exponent.astype(BF16),
                preferred_element_type=F32,
            )
            pieces.append(mixed / row_total)
            lse_ref[head : head + 1, start : start + BLOCK] = peak + jnp.log(row_total)
        out_ref[start : start + BLOCK, :] = jnp.concatenate(pieces, axis=0).T.astype(BF16)


def attend_back_kernel(
    q_ref, k_ref, v_ref, do_ref, lse_ref, seg_col_ref, seg_row_ref, grad_ref, dk_ref, dv_ref
):
    total, width = q_ref.shape
    heads = width // HEAD_DIM
    key_t = k_ref[...].T
    dk_ref[...] = jnp.zeros_like(dk_ref)
    dv_ref[...] = jnp.zeros_like(dv_ref)
    for start in range(0, total, BLOCK):
        keys = start + BLOCK
        bias = mask_bias(seg_col_ref, seg_row_ref, start, keys)
        query = q_ref[start : start + BLOCK, :]
        grad = do_ref[start : start + BLOCK, :]
        pieces = []
        dk = dk_ref[:keys, :]
        dv = dv_ref[:keys, :]
        for head in range(heads):
            lanes = head_lanes(query.shape, head)
            query_h = jnp.where(lanes, query, 0)
            grad_h = jnp.where(lanes, grad, 0)
            scores = contract_cols(k_ref[:keys, :], query_h) + bias
            probs = jnp.exp(scores - lse_ref[head : head + 1, start : start + BLOCK])
            prob_grad = contract_cols(v_ref[:keys, :], grad_h)
            inner = jnp.sum(prob_grad * probs, axis=0, keepdims=True)
            score_grad = (probs * (prob_grad - inner)).astype(BF16)
            dv = dv + jnp.dot(probs.astype(BF16), grad_h, preferred_element_type=F32)
            dk = dk + jnp.dot(score_grad, query_h, preferred_element_type=F32)
            pieces.append(
                jnp.dot(
                    key_t[head * HEAD_DIM : (head + 1) * HEAD_DIM, :keys],
                    score_grad,
                    preferred_element_type=F32,
                )
            )
        dk_ref[:keys, :] = dk
        dv_ref[:keys, :] = dv
        dq = jnp.concatenate(pieces, axis=0).T * HEAD_DIM ** (-0.5)
        grad_ref[start : start + BLOCK, :width] = dq.astype(BF16)
    grad_ref[:, width : 2 * width] = dk_ref[...].astype(BF16)
    grad_ref[:, 2 * width :] = dv_ref[...].astype(BF16)


def whole_specs(count):
    return [pl.BlockSpec(memory_space=pltpu.VMEM) for _ in range(count)]


def attend(query, key, value, seg_col, seg_row):
    total, width = query.shape
    return pl.pallas_call(
        attend_kernel,
        out_shape=(
            jax.ShapeDtypeStruct((total, width), BF16),
            jax.ShapeDtypeStruct((8, total), F32),
        ),
        in_specs=whole_specs(5),
        out_specs=tuple(whole_specs(2)),
        compiler_params=pltpu.CompilerParams(vmem_limit_bytes=48 * 2**20),
        cost_estimate=pl.CostEstimate(
            flops=2 * 2 * total * total * width,
            bytes_accessed=8 * total * width,
            transcendentals=total * total * width // HEAD_DIM // 2,
        ),
    )(query, key, value, seg_col, seg_row)


def attend_back(query, key, value, grad, lse, seg_col, seg_row):
    total, width = query.shape
    return pl.pallas_call(
        attend_back_kernel,
        out_shape=jax.ShapeDtypeStruct((total, 3 * width), BF16),
        in_specs=whole_specs(7),
        out_specs=whole_specs(1)[0],
        scratch_shapes=[pltpu.VMEM((total, width), F32), pltpu.VMEM((total, width), F32)],
        compiler_params=pltpu.CompilerParams(vmem_limit_bytes=48 * 2**20),
        cost_estimate=pl.CostEstimate(
            flops=5 * 2 * total * total * width,
            bytes_accessed=14 * total * width,
            transcendentals=total * total * width // HEAD_DIM // 2,
        ),
    )(query, key, value, grad, lse, seg_col, seg_row)


def local(
    tokens,
    cotangent,
    segments,
    qkv_weight,
    out_weight,
    up_weight,
    down_weight,
    small_weights,
    qkv_first,
    out_first,
    up_first,
    down_first,
    small_first,
    qkv_second,
    out_second,
    up_second,
    down_second,
    small_second,
):
    rep = lax.axis_index("rep")
    shard = lax.axis_index("shard")
    shards = lax.axis_size("shard")
    tok_rows, width = tokens.shape
    part = width // SPAN
    owned = qkv_weight.shape[0]
    ff = up_weight.shape[1]
    unit_rows = down_weight.shape[0]
    units = unit_rows // SPAN
    score_scale = HEAD_DIM ** (-0.5)

    def rep_part(block, size, axis):
        return lax.dynamic_slice_in_dim(block, rep * size, size, axis)

    low_small = small_weights.astype(BF16).T
    low_qkv = rep_part(qkv_weight.astype(BF16).reshape(owned, 3, SPAN, part), 1, 2)
    low_qkv = low_qkv.reshape(owned, 3 * part)
    pad = 64 - low_small.shape[1]
    first_send = jnp.concatenate([low_qkv, jnp.pad(low_small, ((0, 0), (0, pad)))], axis=1)
    low_out = out_weight.astype(BF16)
    low_up = rep_part(up_weight.astype(BF16).reshape(owned, shards, SPAN, units), 1, 2)
    low_up = low_up.reshape(owned, ff // SPAN)
    low_down = rep_part(down_weight, units, 0).astype(BF16)
    first_full = lax.all_gather(first_send, "shard", axis=0, tiled=True)
    out_full = lax.all_gather(low_out, "shard", axis=0, tiled=True)
    up_part = lax.all_gather(low_up, "shard", axis=0, tiled=True)
    down_part = lax.all_gather(low_down, "shard", axis=0, tiled=True)
    qkv_part = first_full[:, : 3 * part]
    small_full = first_full[:, 3 * part : 3 * part + 12].T.astype(F32)
    gain_one, bias_one, query_bias, value_bias, out_bias, gain_two, bias_two, down_bias = (
        small_full[:8]
    )
    up_bias = rep_part(small_full[8:].reshape(shards, SPAN, units), 1, 1).reshape(-1)

    seg_rows = -(-tok_rows // width)
    seg_block = jnp.pad(segments.astype(BF16), (0, seg_rows * width - tok_rows))
    seg_block = jnp.pad(seg_block.reshape(seg_rows, width), ((0, 16 - seg_rows), (0, 0)))
    with_seg = rep_gather(jnp.concatenate([tokens, seg_block], axis=0))
    all_tokens = jnp.concatenate([block[:tok_rows] for block in with_seg], axis=0)
    all_segs = jnp.concatenate(
        [block[tok_rows : tok_rows + seg_rows].reshape(-1)[:tok_rows] for block in with_seg]
    ).astype(jnp.int32)
    seg_col, seg_row = all_segs[:, None], all_segs[None, :]
    all_cot = jnp.concatenate(rep_gather(cotangent), axis=0)

    inputs = all_tokens.astype(F32)
    norm_one, inverse_one = norm_parts(inputs)
    hidden_one = (norm_one * gain_one + bias_one).astype(BF16)
    query_bias_part = rep_part(query_bias, part, 0)
    value_bias_part = rep_part(value_bias, part, 0)
    joined_bias = jnp.concatenate(
        [query_bias_part, jnp.zeros_like(query_bias_part), value_bias_part]
    )
    projected = jnp.dot(hidden_one, qkv_part, preferred_element_type=F32) + joined_bias
    queries = (projected[:, :part] * score_scale).astype(BF16)
    keys = projected[:, part : 2 * part].astype(BF16)
    values = projected[:, 2 * part :].astype(BF16)
    attended_part, log_total = attend(queries, keys, values, seg_col, seg_row)
    attended = jnp.concatenate(rep_gather(attended_part), axis=1)
    residual = inputs + (jnp.dot(attended, out_full, preferred_element_type=F32) + out_bias)
    norm_two, inverse_two = norm_parts(residual)
    hidden_two = (norm_two * gain_two + bias_two).astype(BF16)
    pre_act = jnp.dot(hidden_two, up_part, preferred_element_type=F32) + up_bias
    cdf = 0.5 * (1.0 + lax.erf(pre_act * (0.5**0.5)))
    act_low = (pre_act * cdf).astype(BF16)
    slope = cdf + pre_act * (jnp.exp(-0.5 * pre_act * pre_act) * 0.3989422804014327)
    pre_low = (contract_cols(all_cot, down_part) * slope).astype(BF16)
    hidden_two_grad = rep_scatter(contract_cols(pre_low, up_part))
    mixed_sum = rep_scatter(jnp.dot(act_low, down_part, preferred_element_type=F32))
    residual_own = rep_part(residual, tok_rows, 0)
    mixed = (residual_own + (mixed_sum + down_bias)).astype(BF16)
    down_grad = contract_rows(act_low, all_cot)
    up_grad = contract_rows(hidden_two, pre_low)
    up_bias_grad = jnp.sum(pre_low.astype(F32), axis=0)

    norm_two_own = rep_part(norm_two, tok_rows, 0)
    grad_own = cotangent.astype(F32)
    gain_two_grad = jnp.sum(hidden_two_grad * norm_two_own, axis=0)
    bias_two_grad = jnp.sum(hidden_two_grad, axis=0)
    resid_grad = grad_own + norm_back(
        norm_two_own, rep_part(inverse_two, tok_rows, 0), gain_two, hidden_two_grad
    )
    branch_own = resid_grad.astype(BF16)
    out_bias_grad = jnp.sum(branch_own.astype(F32), axis=0)
    branch_low = jnp.concatenate(rep_gather(branch_own), axis=0)
    out_grad = contract_rows(attended, rep_part(branch_low, part, 1))
    attended_grad = contract_cols(branch_low, rep_part(out_full, part, 0)).astype(BF16)
    proj_low = attend_back(queries, keys, values, attended_grad, log_total, seg_col, seg_row)
    proj_sums = jnp.sum(proj_low.astype(F32), axis=0)
    qkv_grad = contract_rows(hidden_one, proj_low)
    hidden_one_part = contract_cols(proj_low, qkv_part)
    gain_one_grad = jnp.sum(hidden_one_part * norm_one, axis=0)
    bias_one_grad = jnp.sum(hidden_one_part, axis=0)
    hidden_one_grad = rep_scatter(hidden_one_part)
    input_grad = resid_grad + norm_back(
        rep_part(norm_one, tok_rows, 0),
        rep_part(inverse_one, tok_rows, 0),
        gain_one,
        hidden_one_grad,
    )

    def placed(values_part, size, parts_before):
        blank = jnp.zeros((parts_before, SPAN, size), F32)
        return lax.dynamic_update_slice(
            blank, values_part.reshape(parts_before, 1, size), (0, rep, 0)
        ).reshape(-1)

    vector_grads = jnp.stack(
        [
            gain_one_grad,
            bias_one_grad,
            placed(proj_sums[:part], part, 1),
            placed(proj_sums[2 * part :], part, 1),
            out_bias_grad,
            gain_two_grad,
            bias_two_grad,
            jnp.sum(grad_own, axis=0),
        ]
    )
    small_grad = jnp.concatenate(
        [vector_grads, placed(up_bias_grad, units, shards).reshape(-1, width)], axis=0
    )
    small_sum = lax.psum(small_grad, ("rep", "shard"))
    small_own = lax.dynamic_slice_in_dim(
        small_sum, shard * small_weights.shape[1], small_weights.shape[1], 1
    )

    def owned_sum(gradient):
        low = gradient.astype(BF16)
        return rep_gather(lax.psum_scatter(low, "shard", scatter_dimension=0, tiled=True))

    down_own = jnp.concatenate(owned_sum(down_grad), axis=0).astype(F32)
    up_own = jnp.stack([g.reshape(owned, shards, units) for g in owned_sum(up_grad)], axis=2)
    up_own = up_own.reshape(owned, ff).astype(F32)
    out_own = jnp.concatenate(owned_sum(out_grad), axis=1).astype(F32)
    qkv_own = jnp.stack([g.reshape(owned, 3, part) for g in owned_sum(qkv_grad)], axis=2)
    qkv_own = qkv_own.reshape(owned, 3 * width).astype(F32)
    qkv_res = adam_update(qkv_weight, qkv_own, qkv_first, qkv_second, RATE_MATRIX)
    out_res = adam_update(out_weight, out_own, out_first, out_second, RATE_MATRIX)
    up_res = adam_update(up_weight, up_own, up_first, up_second, RATE_MATRIX)
    down_res = adam_update(down_weight, down_own, down_first, down_second, RATE_MATRIX)
    small_res = adam_update(small_weights, small_own, small_first, small_second, RATE_SMALL)
    return (
        mixed,
        input_grad,
        qkv_res[0],
        out_res[0],
        up_res[0],
        down_res[0],
        small_res[0],
        qkv_res[1],
        out_res[1],
        up_res[1],
        down_res[1],
        small_res[1],
        qkv_res[2],
        out_res[2],
        up_res[2],
        down_res[2],
        small_res[2],
    )


def solution(mesh):
    tokens_spec = P(("rep", "shard"), None)
    rows = P("shard", None)
    columns = P(None, "shard")
    weights = (rows, rows, rows, rows, columns)
    return jax.shard_map(
        local,
        mesh=mesh,
        in_specs=(tokens_spec, tokens_spec, P(("rep", "shard"))) + weights * 3,
        out_specs=(tokens_spec, tokens_spec) + weights * 3,
        check_vma=False,
    )
```

time: 971 us -> 477 us (0.49)
  waiting for transfers between devices: 757 us -> 212 us
  matrix products: 79.2 us -> 41.6 us
  blocking collectives: 30.1 us -> 65.7 us
  starting transfers between devices: 20.1 us -> 45.6 us
  Pallas kernels: 0 us -> 13.8 us
  local copies, waits for them, and re-layouts: 17.5 us -> 30.4 us
    reduce_scatter x4, waiting for transfers between devices: 432 us -> 133 us  [owned_sum(): lax.psum_scatter(low, 'shard', scatter_dimension=0, tiled=True)]
    all_gather x4 -> x3, waiting for transfers between devices: 166 us -> 38.4 us  [the longest x1 36.5 us: local(): down_part = lax.all_gather(low_down, 'shard', axis=0, tiled=True)]
    unnamed x11 -> x7, waiting for transfers between devices: 57.3 us -> 0.11 us
    psum x1 -> x0, waiting for transfers between devices: 41.4 us -> none  [local(): lax.psum(owned[0].astype(jnp.bfloat16), 'rep').astype(jnp.float32)]
    psum x1, blocking collectives: 8.08 us -> 38.2 us  [local(): small_sum = lax.psum(small_grad, ('rep', 'shard'))]
    dot_general x11 -> x4, matrix products: 42.8 us -> 15.8 us  [the longest x1 6.06 us: local(): pre_act = jnp.dot(hidden_two, up_part, preferred_element_type=F32) + up_bias]
    ppermute x9 -> x30, starting transfers between devices: 19.6 us -> 44.7 us  [swapped(): return lax.ppermute(block, 'rep', [(i, i ^ bit) for i in range(SPAN)])]
    ppermute x9 -> x30, waiting for transfers between devices: 60.2 us -> 40.3 us  [swapped(): return lax.ppermute(block, 'rep', [(i, i ^ bit) for i in range(SPAN)])]
  transfers between devices with their start and end apart: 19 -> 37, of which waited for: 12 -> 14; matrix products, arithmetic and copies ran while one was open for 11% -> 18% of each run, Pallas kernels for 0% -> 3%
where the time goes in v1:
time: 477 us; the launch traced here: 472 us
  waiting for transfers between devices  212 us (44%)
  blocking collectives  65.7 us (14%)
  other arithmetic  47.5 us (10%)
  starting transfers between devices  45.6 us (10%)
  matrix products  41.6 us (9%)
  local copies, waits for them, and re-layouts  30.4 us (6%)
  between operations  15.4 us (3%)
  Pallas kernels  13.8 us (3%)
    reduce_scatter x4, waiting for transfers between devices, owned_sum(): lax.psum_scatter(low, 'shard', scatter_dimension=0, tiled=True)  133 us
    ppermute x30, starting transfers between devices, swapped(): return lax.ppermute(block, 'rep', [(i, i ^ bit) for i in range(SPAN)])  44.7 us
    ppermute x30, waiting for transfers between devices, swapped(): return lax.ppermute(block, 'rep', [(i, i ^ bit) for i in range(SPAN)])  40.3 us
    psum x1, blocking collectives, local(): small_sum = lax.psum(small_grad, ('rep', 'shard'))  38.2 us
    all_gather x1, waiting for transfers between devices, local(): down_part = lax.all_gather(low_down, 'shard', axis=0, tiled=True)  36.5 us
    all_gather x1, blocking collectives, local(): first_full = lax.all_gather(first_send, 'shard', axis=0, tiled=True)  27.5 us
    dot_general x4, matrix products, contract_cols(): lax.dot_general(left_side, right_side, (((1,), (1,)), ((), ())), preferre...  13.1 us
    dot_general x4, matrix products, contract_rows(): lax.dot_general(left_side, right_side, (((0,), (0,)), ((), ())), preferre...  12.6 us
  transfers between devices with their start and end apart: 37, of which 14 were waited for; matrix products, arithmetic and copies ran while one was open for 18% of the time, Pallas kernels for 3%

profile of v1, /device:TPU:11, one launch (start us, length us, event | category | flops | bytes accessed | tf_op | source)
XLA Modules:
  0.0 471.8 jit_solution(4496581145042341332)
XLA Ops:
  7.2 1.7 convert_element_type.160
  9.7 1.8 fusion.29
  18.1 27.5 %all_gather.12 = bf16[768,640]{1,0:T(8,128)(2,1)S(1)} all-gather(bf16[96,640]{1,0:T(8,128)(2,1)S(1)} %copy.81), channel_id=1, replica_groups=mesh['rep'=4,'shard'=8] {'shard'}, dimensions={0}, use_global_device_ids=true | all-gather | bytes 1105920 | tf_op jit(solution)/shard_map/all_gather | solution.py:259
  45.6 6.3 %collective-permute-start.1 = (bf16[272,768]{1,0:T(8,128)(2,1)}, bf16[272,768]{1,0:T(8,128)(2,1)S(1)}, u32[]{:S(2)}, u32[]{:S(2)}) collective-permute-start(bf16[272,768]{1,0:T(8,128)(2,1)} %collective-permute-done), channel_id=1, source_target_pairs={{0,8},{8,0},{16,24},{24,16},{1,9},{9,1},{17,25},{25,17},{2,10},{10... | collective-permute-start | bytes 1253384 | tf_op jit(solution)/shard_map/ppermute | solution.py:27
  56.7 2.8 fusion.64
  59.8 6.1 %shard_map.305 = (bf16[1024,192]{1,0:T(8,128)(2,1)S(1)}, f32[8,1024]{1,0:T(8,128)S(1)}) custom-call(bf16[1024,192]{1,0:T(8,128)(2,1)S(1)} %fusion.12.q_ref, bf16[1024,192]{1,0:T(8,128)(2,1)S(1)} %get-tuple-element.79.k_ref, bf16[1024,192]{1,0:T(8,128)(2,1)S(1)} %get-tuple-element.78.v_ref, s32[1024,1]{1,0:T(8,128)S(1)} %convert_element_type.158.seg_col_ref, ...), custom_call_target="tpu_custom_call" | custom-call | flops 805306368 | bytes 1572864 | tf_op jit(solution)/shard_map/pallas_call | solution.py:182
  68.9 9.7 %collective-permute-done.3 = bf16[1024,192]{1,0:T(8,128)(2,1)} collective-permute-done((bf16[1024,192]{1,0:T(8,128)(2,1)S(1)}, bf16[1024,192]{1,0:T(8,128)(2,1)}, u32[]{:S(2)}, u32[]{:S(2)}) %collective-permute-start.3) | collective-permute-done | bytes 393248 | tf_op jit(solution)/shard_map/ppermute | solution.py:27
  78.7 1.8 collective-permute-start.4
  84.9 2.7 broadcast_select_fusion.31
  87.6 3.1 broadcast_select_fusion.7
  90.7 3.8 fusion.65
  96.2 2.1 subtract_multiply_fusion
  98.2 1.8 all-gather.6.cloned.1.call-done
  100.1 6.1 %multiply_convert_fusion = (bf16[1024,768]{1,0:T(8,128)(2,1)}, f32[1024,768]{1,0:T(8,128)}) fusion(f32[768]{0:T(1024)S(1)} %add.285, bf16[768,768]{1,0:T(8,128)(2,1)} %all-gather.6.cloned.1.call-done, f32[1024,768]{1,0:T(8,128)} %subtract_multiply_fusion, f32[768]{0:T(1024)S(1)} %get-tuple-element.107, f32[768]{0:T(1024)S(1)} %get-tuple-element.106), kind=kOutput, calls=%fused_computation.15 | convolution fusion | flops 1215037440 | bytes 9053184 | tf_op jit(solution)/shard_map/dot_general | solution.py:298
  106.2 36.5 %all-gather.8.cloned.1.call-done = bf16[768,768]{1,0:T(8,128)(2,1)} async-done(((bf16[96,768]{1,0:T(8,128)(2,1)}), bf16[768,768]{1,0:T(8,128)(2,1)}) %all-gather.8.cloned.1.call-update) | async-done | bytes 1179664 | tf_op jit(solution)/shard_map/all_gather | solution.py:262
  142.7 5.1 %convert_reduce_fusion.1 = (f32[768]{0:T(1024)S(1)}, bf16[1024,768]{1,0:T(8,128)(2,1)S(1)}) fusion(f32[1024,768]{1,0:T(8,128)} %get-tuple-element.120, f32[768]{0:T(1024)S(1)} %add.285, bf16[768,768]{1,0:T(8,128)(2,1)} %all-gather.8.cloned.1.call-done, bf16[256,768]{1,0:T(8,128)(2,1)} %get-tuple-element.77, bf16[256,768]{1,0:T(8,128)(2,1)} %get-tuple-element.76, ...), kind=kOutput, calls=%fused_computation.13 | convolution fusion | flops 1224473856 | bytes 7477248 | tf_op jit(solution)/shard_map/dot_general | solution.py:82
  152.7 2.1 collective-permute-done.11
  158.7 9.2 %collective-permute-done.12 = bf16[256,768]{1,0:T(8,128)(2,1)} collective-permute-done((bf16[256,768]{1,0:T(8,128)(2,1)S(1)}, bf16[256,768]{1,0:T(8,128)(2,1)}, u32[]{:S(2)}, u32[]{:S(2)}) %collective-permute-start.12) | collective-permute-done | bytes 393248 | tf_op jit(solution)/shard_map/ppermute | solution.py:27
  167.8 2.1 multiply_reduce_fusion.2
  170.0 2.4 convert_reduce_fusion.4
  175.1 6.7 %collective-permute-done.13 = bf16[256,768]{1,0:T(8,128)(2,1)S(1)} collective-permute-done((bf16[256,768]{1,0:T(8,128)(2,1)S(1)}, bf16[256,768]{1,0:T(8,128)(2,1)S(1)}, u32[]{:S(2)}, u32[]{:S(2)}) %collective-permute-start.13) | collective-permute-done | bytes 393248 | tf_op jit(solution)/shard_map/ppermute | solution.py:27
  181.9 2.1 collective-permute-start.14
  187.6 1.9 convolution_convert_fusion.3
  189.6 4.0 convolution_convert_fusion
  193.7 3.1 fusion.66
  205.3 3.9 convolution_convert_fusion.1
  211.8 2.7 collective-permute-done.7
  214.5 2.7 fusion.27
  219.1 7.7 %shard_map.306 = bf16[1024,576]{1,0:T(8,128)(2,1)S(1)} custom-call(bf16[1024,192]{1,0:T(8,128)(2,1)S(1)} %fusion.12.q_ref, bf16[1024,192]{1,0:T(8,128)(2,1)S(1)} %get-tuple-element.79.k_ref, bf16[1024,192]{1,0:T(8,128)(2,1)S(1)} %get-tuple-element.78.v_ref, bf16[1024,192]{1,0:T(8,128)(2,1)S(1)} %copy.86.do_ref, f32[8,1024]{1,0:T(8,128)S(1)} %get-tuple-element.20.lse_ref, ...), custom_call_target="tpu_custom_call" | custom-call | flops 2013265920 | bytes 2752512 | tf_op jit(solution)/shard_map/pallas_call | solution.py:201
  226.8 5.0 %fusion.46 = (f32[768]{0:T(1024)S(1)}, f32[768]{0:T(1024)S(1)}, f32[1024,768]{1,0:T(8,128)}, f32[1024,768]{1,0:T(8,128)S(1)}) fusion(f32[1024]{0:T(1024)S(1)} %add_rsqrt_fusion.1, f32[1024]{0:T(1024)S(1)} %broadcast_multiply_fusion.1, bf16[256,768]{1,0:T(8,128)(2,1)S(1)} %copy-done.12, bf16[256,768]{1,0:T(8,128)(2,1)S(1)} %copy-done.14, ...), kind=kOutput, calls=%fused_computation.205 | convolution fusion | flops 916191744 | bytes 10041344 | tf_op jit(solution)/shard_map/dot_general | solution.py:82
  231.8 1.7 copy-done.16
  233.8 2.7 convolution_convert_fusion.2
  236.6 12.1 %reduce-scatter.7.cloned.1.call-done = bf16[96,192]{1,0:T(8,128)(2,1)} async-done(((bf16[768,192]{1,0:T(8,128)(2,1)}), bf16[96,192]{1,0:T(8,128)(2,1)}) %reduce-scatter.7.cloned.1.call-update) | async-done | bytes 36880 | tf_op jit(solution)/shard_map/reduce_scatter | solution.py:365
  250.4 3.3 collective-permute-start.16
  253.8 38.2 %psum.7 = f32[12,768]{1,0:T(8,128)S(1)} all-reduce(f32[12,768]{1,0:T(8,128)S(1)} %concatenate.87), channel_id=1, replica_groups=mesh['rep'=4,'shard'=8] {'rep','shard'}, use_global_device_ids=true, to_apply=%region_20.21 | all-reduce | flops 9216 | bytes 73728 | tf_op jit(solution)/shard_map/psum | solution.py:358
  292.1 24.0 %reduce-scatter.11.cloned.1.call-done = bf16[96,768]{1,0:T(8,128)(2,1)} async-done(((bf16[768,768]{1,0:T(8,128)(2,1)}), bf16[96,768]{1,0:T(8,128)(2,1)}) %reduce-scatter.11.cloned.1.call-update) | async-done | bytes 147472 | tf_op jit(solution)/shard_map/reduce_scatter | solution.py:365
  317.3 65.6 %reduce-scatter.9.cloned.1.call-done = bf16[96,768]{1,0:T(8,128)(2,1)} async-done(((bf16[768,768]{1,0:T(8,128)(2,1)}), bf16[96,768]{1,0:T(8,128)(2,1)}) %reduce-scatter.9.cloned.1.call-update) | async-done | bytes 147472 | tf_op jit(solution)/shard_map/reduce_scatter | solution.py:365
  384.1 2.8 collective-permute-start.23
  388.1 2.7 collective-permute-start.26
  394.9 2.6 reshape.265
  397.6 4.5 multiply_subtract_fusion.1
  406.1 2.4 multiply_subtract_fusion
  408.5 7.2 %collective-permute-done.17 = bf16[256,768]{1,0:T(8,128)(2,1)S(1)} collective-permute-done((bf16[256,768]{1,0:T(8,128)(2,1)S(1)}, bf16[256,768]{1,0:T(8,128)(2,1)S(1)}, u32[]{:S(2)}, u32[]{:S(2)}) %collective-permute-start.17) | collective-permute-done | bytes 393248 | tf_op jit(solution)/shard_map/ppermute | solution.py:27
  417.2 31.3 %reduce-scatter.5.cloned.1.call-done = bf16[96,576]{1,0:T(8,128)(2,1)} async-done(((bf16[768,576]{1,0:T(8,128)(2,1)}), bf16[96,576]{1,0:T(8,128)(2,1)}) %reduce-scatter.5.cloned.1.call-update) | async-done | bytes 110608 | tf_op jit(solution)/shard_map/reduce_scatter | solution.py:365
  449.7 2.9 collective-permute-start.20
  452.5 3.6 collective-permute-start.19
  456.2 2.3 multiply_add_fusion.2
  461.4 3.3 multiply_subtract_fusion.2
  (275 shorter events, 68.4 us)
Async XLA Ops:
  7.2 83.5 %all-gather.4.cloned.1.call-start = ((), (), s32[]{:S(2)}) async-start(), calls=%async_computation.4 | async-start | bytes 1327104 | tf_op jit(solution)/shard_map/all_gather | solution.py:260
  9.0 91.1 %all-gather.6.cloned.1.call-start = ((), (), s32[]{:S(2)}) async-start(), calls=%async_computation.5 | async-start | bytes 1327104 | tf_op jit(solution)/shard_map/all_gather | solution.py:261
  11.5 42.2 %collective-permute-start.2 = (bf16[272,768]{1,0:T(8,128)(2,1)}, bf16[272,768]{1,0:T(8,128)(2,1)S(1)}, u32[]{:S(2)}, u32[]{:S(2)}) collective-permute-start(bf16[272,768]{1,0:T(8,128)(2,1)} %fusion.29), channel_id=1, source_target_pairs={{0,8},{8,0},{16,24},{24,16},{1,9},{9,1},{17,25},{25,17},{2,10},{10... | collective-permute-start | bytes 1253384 | tf_op jit(solution)/shard_map/ppermute | solution.py:27
  12.2 33.4 %collective-permute-start = (bf16[272,768]{1,0:T(8,128)(2,1)}, bf16[272,768]{1,0:T(8,128)(2,1)}, u32[]{:S(2)}, u32[]{:S(2)}) collective-permute-start(bf16[272,768]{1,0:T(8,128)(2,1)} %fusion.29), channel_id=1, source_target_pairs={{0,16},{8,24},{16,0},{24,8},{1,17},{9,25},{17,1},{25,9},{2,18},{10... | collective-permute-start | bytes 1253384 | tf_op jit(solution)/shard_map/ppermute | solution.py:27
  13.4 55.0 %collective-permute-start.8 = (bf16[256,768]{1,0:T(8,128)(2,1)}, bf16[256,768]{1,0:T(8,128)(2,1)}, u32[]{:S(2)}, u32[]{:S(2)}) collective-permute-start(bf16[256,768]{1,0:T(8,128)(2,1)} %param.19), channel_id=1, source_target_pairs={{0,16},{8,24},{16,0},{24,8},{1,17},{9,25},{17,1},{25,9},{2,18},{10... | collective-permute-start | bytes 1179656 | tf_op jit(solution)/shard_map/ppermute | solution.py:27
  16.7 126.1 %all-gather.8.cloned.1.call-start = ((), (), s32[]{:S(2)}) async-start(), calls=%async_computation.6 | async-start | bytes 1327104 | tf_op jit(solution)/shard_map/all_gather | solution.py:262
  45.6 8.1 %collective-permute-start.1 = (bf16[272,768]{1,0:T(8,128)(2,1)}, bf16[272,768]{1,0:T(8,128)(2,1)S(1)}, u32[]{:S(2)}, u32[]{:S(2)}) collective-permute-start(bf16[272,768]{1,0:T(8,128)(2,1)} %collective-permute-done), channel_id=1, source_target_pairs={{0,8},{8,0},{16,24},{24,16},{1,9},{9,1},{17,25},{25,17},{2,10},{10... | collective-permute-start | bytes 1253384 | tf_op jit(solution)/shard_map/ppermute | solution.py:27
  66.0 12.7 %collective-permute-start.3 = (bf16[1024,192]{1,0:T(8,128)(2,1)S(1)}, bf16[1024,192]{1,0:T(8,128)(2,1)}, u32[]{:S(2)}, u32[]{:S(2)}) collective-permute-start(bf16[1024,192]{1,0:T(8,128)(2,1)S(1)} %get-tuple-element.19), channel_id=1, source_target_pairs={{0,16},{8,24},{16,0},{24,8},{1,17},{9,25},{17,1},{25,9},{2,18},{10... | collective-permute-start | bytes 1179656 | tf_op jit(solution)/shard_map/ppermute | solution.py:27
  67.2 17.7 %collective-permute-start.10 = (bf16[256,768]{1,0:T(8,128)(2,1)}, bf16[256,768]{1,0:T(8,128)(2,1)}, u32[]{:S(2)}, u32[]{:S(2)}) collective-permute-start(bf16[256,768]{1,0:T(8,128)(2,1)} %param.19), channel_id=1, source_target_pairs={{0,8},{8,0},{16,24},{24,16},{1,9},{9,1},{17,25},{25,17},{2,10},{10... | collective-permute-start | bytes 1179656 | tf_op jit(solution)/shard_map/ppermute | solution.py:27
  68.4 16.5 %collective-permute-start.9 = (bf16[256,768]{1,0:T(8,128)(2,1)}, bf16[256,768]{1,0:T(8,128)(2,1)}, u32[]{:S(2)}, u32[]{:S(2)}) collective-permute-start(bf16[256,768]{1,0:T(8,128)(2,1)} %collective-permute-done.8), channel_id=1, source_target_pairs={{0,8},{8,0},{16,24},{24,16},{1,9},{9,1},{17,25},{25,17},{2,10},{10... | collective-permute-start | bytes 1179656 | tf_op jit(solution)/shard_map/ppermute | solution.py:27
  68.4 19.2 %collective-permute-start.5 = (bf16[1024,192]{1,0:T(8,128)(2,1)S(1)}, bf16[1024,192]{1,0:T(8,128)(2,1)}, u32[]{:S(2)}, u32[]{:S(2)}) collective-permute-start(bf16[1024,192]{1,0:T(8,128)(2,1)S(1)} %get-tuple-element.19), channel_id=1, source_target_pairs={{0,8},{8,0},{16,24},{24,16},{1,9},{9,1},{17,25},{25,17},{2,10},{10... | collective-permute-start | bytes 1179656 | tf_op jit(solution)/shard_map/ppermute | solution.py:27
  78.7 9.0 %collective-permute-start.4 = (bf16[1024,192]{1,0:T(8,128)(2,1)}, bf16[1024,192]{1,0:T(8,128)(2,1)}, u32[]{:S(2)}, u32[]{:S(2)}) collective-permute-start(bf16[1024,192]{1,0:T(8,128)(2,1)} %collective-permute-done.3), channel_id=1, source_target_pairs={{0,8},{8,0},{16,24},{24,16},{1,9},{9,1},{17,25},{25,17},{2,10},{10... | collective-permute-start | bytes 1179656 | tf_op jit(solution)/shard_map/ppermute | solution.py:27
  82.1 166.6 %reduce-scatter.7.cloned.1.call-start = ((), (), s32[]{:S(2)}) async-start(), calls=%async_computation.8 | async-start | bytes 442368 | tf_op jit(solution)/shard_map/reduce_scatter | solution.py:365
  100.1 42.6 %copy-start.33 = (bf16[256,768]{1,0:T(8,128)(2,1)S(1)}, bf16[256,768]{1,0:T(8,128)(2,1)}, u32[]{:S(2)}) copy-start(bf16[256,768]{1,0:T(8,128)(2,1)} %get-tuple-element.74) | copy-start | bytes 1179652
  100.1 42.6 %copy-start.35 = (bf16[256,768]{1,0:T(8,128)(2,1)S(1)}, bf16[256,768]{1,0:T(8,128)(2,1)}, u32[]{:S(2)}) copy-start(bf16[256,768]{1,0:T(8,128)(2,1)} %get-tuple-element.75) | copy-start | bytes 1179652
  151.2 3.7 collective-permute-start.11
  157.3 10.5 %collective-permute-start.12 = (bf16[256,768]{1,0:T(8,128)(2,1)S(1)}, bf16[256,768]{1,0:T(8,128)(2,1)}, u32[]{:S(2)}, u32[]{:S(2)}) collective-permute-start(bf16[256,768]{1,0:T(8,128)(2,1)S(1)} %fusion.21), channel_id=1, source_target_pairs={{0,16},{8,24},{16,0},{24,8},{1,17},{9,25},{17,1},{25,9},{2,18},{10... | collective-permute-start | bytes 1179656 | tf_op jit(solution)/shard_map/ppermute | solution.py:27
  172.4 9.4 %collective-permute-start.13 = (bf16[256,768]{1,0:T(8,128)(2,1)S(1)}, bf16[256,768]{1,0:T(8,128)(2,1)S(1)}, u32[]{:S(2)}, u32[]{:S(2)}) collective-permute-start(bf16[256,768]{1,0:T(8,128)(2,1)S(1)} %get-tuple-element.39), channel_id=1, source_target_pairs={{0,16},{8,24},{16,0},{24,8},{1,17},{9,25},{17,1},{25,9},{2,18},{10... | collective-permute-start | bytes 1179656 | tf_op jit(solution)/shard_map/ppermute | solution.py:27
  173.6 10.3 %collective-permute-start.15 = (bf16[256,768]{1,0:T(8,128)(2,1)S(1)}, bf16[256,768]{1,0:T(8,128)(2,1)S(1)}, u32[]{:S(2)}, u32[]{:S(2)}) collective-permute-start(bf16[256,768]{1,0:T(8,128)(2,1)S(1)} %get-tuple-element.39), channel_id=1, source_target_pairs={{0,8},{8,0},{16,24},{24,16},{1,9},{9,1},{17,25},{25,17},{2,10},{10... | collective-permute-start | bytes 1179656 | tf_op jit(solution)/shard_map/ppermute | solution.py:27
  181.9 3.5 collective-permute-start.14
  189.5 126.5 %reduce-scatter.11.cloned.1.call-start = ((), (), s32[]{:S(2)}) async-start(), calls=%async_computation.10 | async-start | bytes 1327104 | tf_op jit(solution)/shard_map/reduce_scatter | solution.py:365
  193.7 189.2 %reduce-scatter.9.cloned.1.call-start = ((), (), s32[]{:S(2)}) async-start(), calls=%async_computation.9 | async-start | bytes 1327104 | tf_op jit(solution)/shard_map/reduce_scatter | solution.py:365
  198.8 2.5 collective-permute-start.6
  204.0 10.5 %collective-permute-start.7 = (bf16[256,768]{1,0:T(8,128)(2,1)S(1)}, bf16[256,768]{1,0:T(8,128)(2,1)S(1)}, u32[]{:S(2)}, u32[]{:S(2)}) collective-permute-start(bf16[256,768]{1,0:T(8,128)(2,1)S(1)} %fusion.23), channel_id=1, source_target_pairs={{0,16},{8,24},{16,0},{24,8},{1,17},{9,25},{17,1},{25,9},{2,18},{10... | collective-permute-start | bytes 1179656 | tf_op jit(solution)/shard_map/ppermute | solution.py:27
  209.3 239.3 %reduce-scatter.5.cloned.1.call-start = ((), (), s32[]{:S(2)}) async-start(), calls=%async_computation.7 | async-start | bytes 1105920 | tf_op jit(solution)/shard_map/reduce_scatter | solution.py:365
  236.6 150.4 %copy-start.44 = (f32[12,96]{1,0:T(8,128)S(1)}, f32[12,96]{1,0:T(8,128)}, u32[]{:S(2)}) copy-start(f32[12,96]{1,0:T(8,128)} %param.25) | copy-start | bytes 13828
  236.6 150.4 %copy-start.49 = (f32[12,96]{1,0:T(8,128)S(1)}, f32[12,96]{1,0:T(8,128)}, u32[]{:S(2)}) copy-start(f32[12,96]{1,0:T(8,128)} %param.30) | copy-start | bytes 13828
  236.6 150.4 %copy-start.50 = (f32[12,96]{1,0:T(8,128)S(1)}, f32[12,96]{1,0:T(8,128)}, u32[]{:S(2)}) copy-start(f32[12,96]{1,0:T(8,128)} %param.35) | copy-start | bytes 13828
  248.7 135.4 %copy-start.42 = (bf16[96,192]{1,0:T(8,128)(2,1)S(1)}, bf16[96,192]{1,0:T(8,128)(2,1)}, u32[]{:S(2)}) copy-start(bf16[96,192]{1,0:T(8,128)(2,1)} %reduce-scatter.7.cloned.1.call-done) | copy-start | bytes 110596
  248.7 138.2 %collective-permute-start.21 = (bf16[96,192]{1,0:T(8,128)(2,1)}, bf16[96,192]{1,0:T(8,128)(2,1)S(1)}, u32[]{:S(2)}, u32[]{:S(2)}) collective-permute-start(bf16[96,192]{1,0:T(8,128)(2,1)} %reduce-scatter.7.cloned.1.call-done), channel_id=1, source_target_pairs={{0,16},{8,24},{16,0},{24,8},{1,17},{9,25},{17,1},{25,9},{2,18},{10... | collective-permute-start | bytes 110600 | tf_op jit(solution)/shard_map/ppermute | solution.py:27
  249.9 141.4 %copy-start.26 = (f32[96,768]{1,0:T(8,128)S(1)}, f32[96,768]{1,0:T(8,128)}, u32[]{:S(2)}) copy-start(f32[96,768]{1,0:T(8,128)} %param.22) | copy-start | bytes 884740
  249.9 141.4 %copy-start.37 = (f32[96,768]{1,0:T(8,128)S(1)}, f32[96,768]{1,0:T(8,128)}, u32[]{:S(2)}) copy-start(f32[96,768]{1,0:T(8,128)} %param.27) | copy-start | bytes 884740
  249.9 141.4 %copy-start.38 = (f32[96,768]{1,0:T(8,128)S(1)}, f32[96,768]{1,0:T(8,128)}, u32[]{:S(2)}) copy-start(f32[96,768]{1,0:T(8,128)} %param.32) | copy-start | bytes 884740
  250.4 153.0 %collective-permute-start.16 = (bf16[512,768]{1,0:T(8,128)(2,1)S(1)}, bf16[512,768]{1,0:T(8,128)(2,1)}, u32[]{:S(2)}, u32[]{:S(2)}) collective-permute-start(bf16[512,768]{1,0:T(8,128)(2,1)S(1)} %pad_maximum_fusion.6), channel_id=1, source_target_pairs={{0,8},{8,0},{16,24},{24,16},{1,9},{9,1},{17,25},{25,17},{2,10},{10... | collective-permute-start | bytes 2359304 | tf_op jit(solution)/shard_map/ppermute | solution.py:27
  316.0 71.6 %collective-permute-start.27 = (bf16[96,768]{1,0:T(8,128)(2,1)}, bf16[96,768]{1,0:T(8,128)(2,1)}, u32[]{:S(2)}, u32[]{:S(2)}) collective-permute-start(bf16[96,768]{1,0:T(8,128)(2,1)} %reduce-scatter.11.cloned.1.call-done), channel_id=1, source_target_pairs={{0,16},{8,24},{16,0},{24,8},{1,17},{9,25},{17,1},{25,9},{2,18},{10... | collective-permute-start | bytes 442376 | tf_op jit(solution)/shard_map/ppermute | solution.py:27
  382.9 5.2 %collective-permute-start.24 = (bf16[96,768]{1,0:T(8,128)(2,1)}, bf16[96,768]{1,0:T(8,128)(2,1)S(1)}, u32[]{:S(2)}, u32[]{:S(2)}) collective-permute-start(bf16[96,768]{1,0:T(8,128)(2,1)} %reduce-scatter.9.cloned.1.call-done), channel_id=1, source_target_pairs={{0,16},{8,24},{16,0},{24,8},{1,17},{9,25},{17,1},{25,9},{2,18},{10... | collective-permute-start | bytes 442376 | tf_op jit(solution)/shard_map/ppermute | solution.py:27
  384.1 6.7 %collective-permute-start.23 = (bf16[96,192]{1,0:T(8,128)(2,1)S(1)}, bf16[96,192]{1,0:T(8,128)(2,1)S(1)}, u32[]{:S(2)}, u32[]{:S(2)}) collective-permute-start(bf16[96,192]{1,0:T(8,128)(2,1)S(1)} %copy-done.42), channel_id=1, source_target_pairs={{0,8},{8,0},{16,24},{24,16},{1,9},{9,1},{17,25},{25,17},{2,10},{10... | collective-permute-start | bytes 110600 | tf_op jit(solution)/shard_map/ppermute | solution.py:27
  386.9 3.9 collective-permute-start.22
  387.7 14.4 %collective-permute-start.29 = (bf16[96,768]{1,0:T(8,128)(2,1)}, bf16[96,768]{1,0:T(8,128)(2,1)}, u32[]{:S(2)}, u32[]{:S(2)}) collective-permute-start(bf16[96,768]{1,0:T(8,128)(2,1)} %reduce-scatter.11.cloned.1.call-done), channel_id=1, source_target_pairs={{0,8},{8,0},{16,24},{24,16},{1,9},{9,1},{17,25},{25,17},{2,10},{10... | collective-permute-start | bytes 442376 | tf_op jit(solution)/shard_map/ppermute | solution.py:27
  388.1 4.4 collective-permute-start.26
  390.8 11.3 %collective-permute-start.28 = (bf16[96,768]{1,0:T(8,128)(2,1)}, bf16[96,768]{1,0:T(8,128)(2,1)}, u32[]{:S(2)}, u32[]{:S(2)}) collective-permute-start(bf16[96,768]{1,0:T(8,128)(2,1)} %collective-permute-done.27), channel_id=1, source_target_pairs={{0,8},{8,0},{16,24},{24,16},{1,9},{9,1},{17,25},{25,17},{2,10},{10... | collective-permute-start | bytes 442376 | tf_op jit(solution)/shard_map/ppermute | solution.py:27
  390.8 1.8 collective-permute-start.25
  404.9 10.9 %collective-permute-start.17 = (bf16[256,768]{1,0:T(8,128)(2,1)S(1)}, bf16[256,768]{1,0:T(8,128)(2,1)S(1)}, u32[]{:S(2)}, u32[]{:S(2)}) collective-permute-start(bf16[256,768]{1,0:T(8,128)(2,1)S(1)} %fusion.18), channel_id=1, source_target_pairs={{0,16},{8,24},{16,0},{24,8},{1,17},{9,25},{17,1},{25,9},{2,18},{10... | collective-permute-start | bytes 1179656 | tf_op jit(solution)/shard_map/ppermute | solution.py:27
  415.7 40.5 %copy-start.15 = (f32[256,768]{1,0:T(8,128)S(1)}, f32[256,768]{1,0:T(8,128)}, u32[]{:S(2)}) copy-start(f32[256,768]{1,0:T(8,128)} %get-tuple-element.40) | copy-start | bytes 2359300
  415.7 40.5 %copy-start.51 = (f32[256]{0:T(256)S(1)}, f32[256]{0:T(256)}, u32[]{:S(2)}) copy-start(f32[256]{0:T(256)} %dynamic-slice.9) | copy-start | bytes 3076
  448.5 4.0 collective-permute-start.18
  449.7 8.8 %collective-permute-start.20 = (bf16[96,576]{1,0:T(8,128)(2,1)}, bf16[96,576]{1,0:T(8,128)(2,1)S(1)}, u32[]{:S(2)}, u32[]{:S(2)}) collective-permute-start(bf16[96,576]{1,0:T(8,128)(2,1)} %reduce-scatter.5.cloned.1.call-done), channel_id=1, source_target_pairs={{0,8},{8,0},{16,24},{24,16},{1,9},{9,1},{17,25},{25,17},{2,10},{10... | collective-permute-start | bytes 331784 | tf_op jit(solution)/shard_map/ppermute | solution.py:27
  452.5 5.9 %collective-permute-start.19 = (bf16[96,576]{1,0:T(8,128)(2,1)S(1)}, bf16[96,576]{1,0:T(8,128)(2,1)S(1)}, u32[]{:S(2)}, u32[]{:S(2)}) collective-permute-start(bf16[96,576]{1,0:T(8,128)(2,1)S(1)} %collective-permute-done.18), channel_id=1, source_target_pairs={{0,8},{8,0},{16,24},{24,16},{1,9},{9,1},{17,25},{25,17},{2,10},{10... | collective-permute-start | bytes 331784 | tf_op jit(solution)/shard_map/ppermute | solution.py:27
  (43 other events, 197.6 us)
Sparse Core Ops, SparseCore 0:
  10.8 47.8 all-gather.3
  61.5 38.5 all-gather.5
  102.9 39.7 all-gather.7
  189.6 59.0 reduce-scatter.6
  252.5 63.4 reduce-scatter.10
  319.8 62.9 reduce-scatter.8
  386.2 62.2 reduce-scatter.4
